TPU v7x, 32 devices: a whole 2x2x4 slice. The times are simulated.
32 devices in a mesh: ctx: 8 (over y, x, core), exp: 4 (over z).
Axes of the slice: x: 2, y: 2, z: 4, core: 2. Of those that a mesh axis runs over, the one named last changes fastest.
Arguments:
- inputs: bfloat16 [1024, 1024], P('exp', 'ctx'), may hold values from -6 to 6
- conv_taps: float32 [1024, 31], P('exp'), may hold values from -1 to 1
- norm_gain: bfloat16 [1024], P('exp'), may hold values from 0.099609375 to 1.8984375
- routes: int32 [1024, 2], P('ctx'), may hold values from 0 to 7, all different within a row; in each aligned block of 128 rows (0 to 127, 128 to 255, ...) at most 32 rows name the same one
- gate_probs: float32 [1024, 2], P('ctx'), may hold values from 0.1 to 0.9
- w_gate: bfloat16 [8, 1024, 4096], P('ctx', None, 'exp'), may hold values from -0.1875 to 0.1875
- w_up: bfloat16 [8, 1024, 4096], P('ctx', None, 'exp'), may hold values from -0.1875 to 0.1875
- w_down: bfloat16 [8, 4096, 1024], P('ctx', 'exp'), may hold values from -0.09375 to 0.09375
- grad_out: bfloat16 [1024, 1024], P('exp', 'ctx'), may hold values from -6 to 6
Outputs:
- layer_out: bfloat16 [1024, 1024], P('exp', 'ctx')
- grad_inputs: bfloat16 [1024, 1024], P('exp', 'ctx')
- grad_taps: float32 [1024, 31], P('exp')
- grad_gain: float32 [1024], P('exp')
- grad_gates: float32 [1024, 2], P('ctx')
- grad_w_gate: bfloat16 [8, 1024, 4096], P('ctx', None, 'exp')
- grad_w_up: bfloat16 [8, 1024, 4096], P('ctx', None, 'exp')
- grad_w_down: bfloat16 [8, 4096, 1024], P('ctx', 'exp')
Inputs may be any that keep to these rules, and one draw needn't show every extreme that they name: `routes`: in each aligned block of 128 rows (the rows of one index of ctx) no expert is named by more than 32 rows, a bound that some block reaches; the two experts of a row differ.
All inputs are finite; a program needn't handle non-finite values.
Results may differ from a plain program's by a relative error of at most 0.025.
Values may be sent and summed in bfloat16 or wider, within the bound.
A program may use at most 64 MiB of HBM per device.

v0:
```python
import jax
import jax.numpy as jnp
from jax import lax
from jax.sharding import PartitionSpec as P

EPS = 1e-05


def padded_2(cells, sides, width):
    for axis, dim in sides:
        count = lax.axis_size(axis)
        head = lax.slice_in_dim(cells, 0, width, axis=dim)
        tail = lax.slice_in_dim(cells, cells.shape[dim] - width, cells.shape[dim], axis=dim)
        cells = jnp.concatenate(
            [
                lax.ppermute(tail, axis, [(i, (i + 1) % count) for i in range(count)]),
                cells,
                lax.ppermute(head, axis, [((i + 1) % count, i) for i in range(count)]),
            ],
            axis=dim,
        )
    return cells


def shortened(x):

    def short(part):
        return part.astype(jnp.bfloat16) if part.dtype == jnp.float32 else part

    return jax.tree.map(short, x)


def slot_rows(routes, experts, capacity):
    flat = routes.reshape(-1)
    onehot = (flat[:, None] == jnp.arange(experts, dtype=jnp.int32)[None, :]).astype(jnp.int32)
    before = jnp.cumsum(onehot, axis=0, dtype=jnp.int32) - onehot
    place = jnp.sum(before * onehot, axis=1, dtype=jnp.int32)
    return flat * capacity + place


def bring_back(values, dest, weights, experts, capacity, whole_cot):
    width = values.shape[1]
    back = lax.all_to_all(
        values.reshape(experts, capacity, width).astype(jnp.bfloat16),
        "ctx",
        split_axis=0,
        concat_axis=0,
        tiled=True,
    ).astype(jnp.float32)
    picked = back.reshape(experts * capacity, width)[dest]
    term = jnp.sum((picked * weights[:, None]).reshape(-1, 2, width), axis=1)
    share = lax.psum_scatter(
        term.astype(jnp.bfloat16), "exp", scatter_dimension=1, tiled=True
    ).astype(jnp.float32)
    dots = None if whole_cot is None else jnp.sum(picked * whole_cot, axis=1)
    return (share, dots)


def local(inputs, conv_taps, norm_gain, routes, gate_probs, w_gate, w_up, w_down, grad_out):
    chans, tokens = inputs.shape
    taps = conv_taps.shape[1]
    half = taps // 2
    width = w_gate.shape[1]
    experts = lax.axis_size("ctx")
    capacity = max(tokens // 8, (2 * tokens + experts - 1) // experts)
    padded = padded_2(inputs, (("ctx", 1),), half)
    padded_f = padded.astype(jnp.float32)
    conv = jnp.zeros((chans, tokens), jnp.float32)
    for offset in range(taps):
        conv = conv + conv_taps[:, offset : offset + 1] * padded_f[:, offset : offset + tokens]
    mixed = (inputs.astype(jnp.float32) + conv).astype(jnp.bfloat16)
    mixed_f = mixed.astype(jnp.float32)
    gain_f = norm_gain.astype(jnp.float32)
    squares = lax.psum(jnp.sum(mixed_f * mixed_f, axis=0), "exp")
    scale = lax.rsqrt(squares / width + EPS)
    normed_part = (mixed_f * gain_f[:, None] * scale[None, :]).astype(jnp.bfloat16)
    normed, cotangent = (
        lax.all_gather(normed_part, "exp", axis=0, tiled=True),
        lax.all_gather(grad_out, "exp", axis=0, tiled=True),
    )
    dest = slot_rows(routes, experts, capacity)
    gates = gate_probs.reshape(-1)
    cot_rows = jnp.repeat(cotangent.T, 2, axis=0).astype(jnp.float32)
    token_rows = jnp.repeat(normed.T, 2, axis=0)
    scaled_rows = (cot_rows * gates[:, None]).astype(jnp.bfloat16)
    empty = jnp.zeros((experts * capacity, width), jnp.bfloat16)
    send_x = empty.at[dest].set(token_rows).reshape(experts, capacity, width)
    send_dy = empty.at[dest].set(scaled_rows).reshape(experts, capacity, width)
    recv_x, recv_dy = (
        lax.all_to_all(send_x, "ctx", split_axis=0, concat_axis=0, tiled=True),
        lax.all_to_all(send_dy, "ctx", split_axis=0, concat_axis=0, tiled=True),
    )
    rows_x = recv_x.reshape(-1, width)
    rows_dy = recv_dy.reshape(-1, width)
    weight_gate = w_gate[0]
    weight_up = w_up[0]
    weight_down = w_down[0]
    gate_act = jnp.dot(rows_x, weight_gate, preferred_element_type=jnp.float32)
    up_act = jnp.dot(rows_x, weight_up, preferred_element_type=jnp.float32)
    sigma = jax.nn.sigmoid(gate_act)
    hidden = (gate_act * sigma * up_act).astype(jnp.bfloat16)
    partial_out = jnp.dot(hidden, weight_down, preferred_element_type=jnp.float32)
    moe_share, gate_dots = bring_back(partial_out, dest, gates, experts, capacity, cot_rows)
    layer_out = (mixed_f + moe_share.T).astype(jnp.bfloat16)
    grad_gates = lax.psum(gate_dots, "exp").reshape(tokens, 2)
    contract_last = (((1,), (1,)), ((), ()))
    contract_first = (((0,), (0,)), ((), ()))
    d_hidden = lax.dot_general(
        rows_dy, weight_down, contract_last, preferred_element_type=jnp.float32
    )
    grad_down = lax.dot_general(
        hidden, rows_dy, contract_first, preferred_element_type=jnp.float32
    ).astype(jnp.bfloat16)
    d_gate = (d_hidden * up_act * sigma * (1.0 + gate_act * (1.0 - sigma))).astype(jnp.bfloat16)
    d_up = (d_hidden * gate_act * sigma).astype(jnp.bfloat16)
    grad_gate = lax.dot_general(
        rows_x, d_gate, contract_first, preferred_element_type=jnp.float32
    ).astype(jnp.bfloat16)
    grad_up = lax.dot_general(
        rows_x, d_up, contract_first, preferred_element_type=jnp.float32
    ).astype(jnp.bfloat16)
    d_rows = lax.dot_general(d_gate, weight_gate, contract_last, preferred_element_type=jnp.float32)
    d_rows = d_rows + lax.dot_general(
        d_up, weight_up, contract_last, preferred_element_type=jnp.float32
    )
    d_share, unused_dots = bring_back(d_rows, dest, jnp.ones_like(gates), experts, capacity, None)
    d_normed = d_share.T
    gain_local = jnp.sum(d_normed * mixed_f * scale[None, :], axis=1)
    norm_terms = lax.psum(jnp.sum(d_normed * gain_f[:, None] * mixed_f, axis=0), "exp")
    cot_own = grad_out.astype(jnp.float32)
    d_mixed = (
        cot_own
        + gain_f[:, None] * d_normed * scale[None, :]
        - mixed_f * (norm_terms * scale * scale * scale / width)[None, :]
    )
    grad_padded = padded_2(shortened(d_mixed), (("ctx", 1),), half).astype(d_mixed.dtype)
    grad_in = d_mixed
    tap_parts = []
    for offset in range(taps):
        grad_in = (
            grad_in
            + conv_taps[:, offset : offset + 1]
            * grad_padded[:, 2 * half - offset : 2 * half - offset + tokens]
        )
        tap_parts.append(jnp.sum(d_mixed * padded_f[:, offset : offset + tokens], axis=1))
    tap_local = jnp.stack(tap_parts, axis=1)
    grad_taps, grad_gain = lax.psum((tap_local, gain_local), "ctx")
    return (
        layer_out,
        grad_in.astype(jnp.bfloat16),
        grad_taps,
        grad_gain,
        grad_gates,
        grad_gate[None],
        grad_up[None],
        grad_down[None],
    )


def solution(mesh):
    return jax.shard_map(
        local,
        mesh=mesh,
        in_specs=(
            P("exp", "ctx"),
            P("exp", None),
            P("exp"),
            P("ctx", None),
            P("ctx", None),
            P("ctx", None, "exp"),
            P("ctx", None, "exp"),
            P("ctx", "exp", None),
            P("exp", "ctx"),
        ),
        out_specs=(
            P("exp", "ctx"),
            P("exp", "ctx"),
            P("exp", None),
            P("exp"),
            P("ctx", None),
            P("ctx", None, "exp"),
            P("ctx", None, "exp"),
            P("ctx", "exp", None),
        ),
        check_vma=False,
    )
```

profile of v0, /device:TPU:0, one launch (start us, length us, event | category | flops | bytes accessed | tf_op | source)
XLA Modules:
  0.0 213.7 jit_solution(18306011151170475799)
XLA Ops:
  8.8 2.9 %collective-permute-start.1 = (bf16[256,15]{0,1:T(8,128)(2,1)S(1)}, bf16[256,15]{0,1:T(8,128)(2,1)S(1)}, u32[]{:S(2)}, u32[]{:S(2)}) collective-permute-start(bf16[256,15]{0,1:T(8,128)(2,1)S(1)} %get-tuple-element.72), channel_id=1, source_target_pairs={{4,0},{8,4},{12,8},{16,12},{20,16},{24,20},{28,24},{0,28},{5,1},{9... | collective-permute-start | bytes 23048 | tf_op jit(solution)/shard_map/ppermute | solution.py:18
  15.5 15.0 %all_gather.7 = bf16[1024,128]{1,0:T(8,128)(2,1)S(1)} all-gather(bf16[256,128]{1,0:T(8,128)(2,1)} %param.17), channel_id=1, replica_groups=mesh['ctx'=8,'exp'=4] {'exp'}, dimensions={0}, use_global_device_ids=true | all-gather | bytes 327680 | tf_op jit(solution)/shard_map/all_gather | solution.py:79
  34.2 2.5 %scatter_custom_fusion.1 = bf16[256,1024]{1,0:T(8,128)(2,1)} fusion(s32[256]{0:T(256)S(1)} %bitcast.245, f32[256,1024]{1,0:T(8,128)S(1)} %convert_element_type.108, f32[256]{0:T(256)S(1)} %mul.828, bf16[]{:T(256)} %constant.8.clone.1), kind=kCustom, calls=%fused_computation.29 | custom fusion | flops 524288 | bytes 1573890 | tf_op jit(solution)/shard_map/scatter | solution.py:88
  36.7 4.1 %all-to-all-start.2 = ((bf16[8,32,1024]{2,1,0:T(8,128)(2,1)}), bf16[8,32,1024]{2,1,0:T(8,128)(2,1)}, u32[]{:S(2)}, u32[]{:S(2)}) async-start(bf16[8,32,1024]{2,1,0:T(8,128)(2,1)} %bitcast.149), calls=%async_computation.3 | async-start | bytes 1048576 | tf_op jit(solution)/shard_map/all_to_all | solution.py:91
  42.4 11.9 %psum.35 = f32[128]{0:T(128)S(1)} all-reduce(f32[128]{0:T(128)} %get-tuple-element.62), channel_id=1, replica_groups=mesh['ctx'=8,'exp'=4] {'exp'}, use_global_device_ids=true, to_apply=%region_4.5 | all-reduce | flops 128 | bytes 1024 | tf_op jit(solution)/shard_map/psum | solution.py:74
  54.9 13.8 %all_gather.6 = bf16[1024,128]{0,1:T(8,128)(2,1)S(1)} all-gather(bf16[256,128]{0,1:T(8,128)(2,1)S(1)} %fusion.27), channel_id=1, replica_groups=mesh['ctx'=8,'exp'=4] {'exp'}, dimensions={0}, use_global_device_ids=true | all-gather | bytes 327680 | tf_op jit(solution)/shard_map/all_gather | solution.py:78
  69.2 2.6 %scatter_custom_fusion = bf16[256,1024]{1,0:T(8,128)(2,1)} fusion(s32[256]{0:T(256)} %bitcast.246, bf16[256,1024]{1,0:T(8,128)(2,1)S(1)} %reshape.158, bf16[]{:T(256)} %constant.8.clone.1), kind=kCustom, calls=%fused_computation.41 | custom fusion | bytes 524800 | tf_op jit(solution)/shard_map/scatter | solution.py:87
  71.8 4.1 %all-to-all-start = ((bf16[8,32,1024]{2,1,0:T(8,128)(2,1)}), bf16[8,32,1024]{2,1,0:T(8,128)(2,1)S(1)}, u32[]{:S(2)}, u32[]{:S(2)}) async-start(bf16[8,32,1024]{2,1,0:T(8,128)(2,1)} %bitcast.36), calls=%async_computation | async-start | bytes 1048576 | tf_op jit(solution)/shard_map/all_to_all | solution.py:90
  76.5 3.5 %fusion.2 = f32[256,1024]{1,0:T(8,128)} fusion(bf16[256,1024]{1,0:T(8,128)(2,1)} %bitcast.47, bf16[1,1024,1024]{2,1,0:T(8,128)(2,1)} %param.16), kind=kOutput, calls=%fused_computation.6 | convolution fusion | flops 536870912 | bytes 3670016 | tf_op jit(solution)/shard_map/dot_general | solution.py:108
  80.0 5.6 %all-to-all-done = bf16[8,32,1024]{2,1,0:T(8,128)(2,1)S(1)} async-done(((bf16[8,32,1024]{2,1,0:T(8,128)(2,1)}), bf16[8,32,1024]{2,1,0:T(8,128)(2,1)S(1)}, u32[]{:S(2)}, u32[]{:S(2)}) %all-to-all-start) | async-done | bytes 524320 | tf_op jit(solution)/shard_map/all_to_all | solution.py:90
  85.6 2.5 %fusion.6 = f32[256,1024]{1,0:T(8,128)S(1)} fusion(bf16[256,1024]{1,0:T(8,128)(2,1)S(1)} %bitcast.145, bf16[1,1024,1024]{2,1,0:T(8,128)(2,1)} %param.15), kind=kOutput, calls=%fused_computation.10 | convolution fusion | flops 536870912 | bytes 3670016 | tf_op jit(solution)/shard_map/dot_general | solution.py:99
  92.5 3.5 %all-to-all-start.1 = ((bf16[8,32,1024]{2,1,0:T(8,128)(2,1)}), bf16[8,32,1024]{2,1,0:T(8,128)(2,1)S(1)}, u32[]{:S(2)}, u32[]{:S(2)}) async-start(bf16[8,32,1024]{2,1,0:T(8,128)(2,1)} %fusion.15), calls=%async_computation.1 | async-start | bytes 1048576 | tf_op jit(solution)/shard_map/all_to_all | solution.py:43
  96.0 2.4 %fusion.4 = f32[256,1024]{1,0:T(8,128)S(1)} fusion(bf16[256,1024]{1,0:T(8,128)(2,1)S(1)} %get-tuple-element.66, bf16[1,1024,1024]{2,1,0:T(8,128)(2,1)} %param.15), kind=kOutput, calls=%fused_computation.8 | convolution fusion | flops 536870912 | bytes 3670016 | tf_op jit(solution)/shard_map/dot_general | solution.py:123
  100.0 5.7 %all-to-all-done.1 = bf16[8,32,1024]{2,1,0:T(8,128)(2,1)S(1)} async-done(((bf16[8,32,1024]{2,1,0:T(8,128)(2,1)}), bf16[8,32,1024]{2,1,0:T(8,128)(2,1)S(1)}, u32[]{:S(2)}, u32[]{:S(2)}) %all-to-all-start.1) | async-done | bytes 524320 | tf_op jit(solution)/shard_map/all_to_all | solution.py:43
  105.6 4.2 %all-to-all-start.3 = ((bf16[8,32,1024]{2,1,0:T(8,128)(2,1)}), bf16[8,32,1024]{2,1,0:T(8,128)(2,1)}, u32[]{:S(2)}, u32[]{:S(2)}) async-start(bf16[8,32,1024]{2,1,0:T(8,128)(2,1)} %bitcast.48), calls=%async_computation.4 | async-start | bytes 1048576 | tf_op jit(solution)/shard_map/all_to_all | solution.py:43
  113.3 2.9 %gather.9 = f32[128,2,1024]{2,1,0:T(2,128)} reshape(f32[256,1024]{1,0:T(8,128)} %gather_fusion) | data formatting | bytes 2097152 | tf_op jit(solution)/shard_map/gather | solution.py:50
  116.2 3.3 %multiply_reduce_fusion.1 = bf16[128,1024]{1,0:T(8,128)(2,1)} fusion(f32[128,2,1024]{2,1,0:T(2,128)} %gather.9, f32[128,2]{1,0:T(8,128)S(1)} %copy.35), kind=kLoop, calls=%fused_computation.26 | loop fusion | flops 393216 | bytes 1311744 | tf_op jit(solution)/shard_map/reduce_sum | solution.py:51
  125.0 2.9 %reshape.132 = f32[128,2,1024]{2,1,0:T(2,128)} reshape(f32[256,1024]{1,0:T(8,128)} %gather_fusion.1) | data formatting | bytes 2097152 | tf_op jit(solution)/shard_map/reshape | solution.py:51
  127.9 3.2 %reduce_sum.348 = bf16[128,1024]{1,0:T(8,128)(2,1)} reduce(f32[128,2,1024]{2,1,0:T(2,128)} %reshape.132, f32[]{:T(128)} %constant.7.clone.1), dimensions={1}, to_apply=%region_9.10 | reduce | flops 131072 | bytes 1310724 | tf_op jit(solution)/shard_map/reduce_sum | solution.py:51
  133.2 3.3 %convert_bitcast_fusion = bf16[1,1024,1024]{2,1,0:T(8,128)(2,1)} fusion(bf16[256,1024]{1,0:T(8,128)(2,1)S(1)} %copy-done.15, bf16[256,1024]{1,0:T(8,128)(2,1)} %bitcast.47), kind=kOutput, calls=%fused_computation.16 | convolution fusion | flops 537919488 | bytes 3145728 | tf_op jit(solution)/shard_map/dot_general | solution.py:111
  137.8 20.4 %reduce-scatter.5.cloned.1.call-done = bf16[128,256]{1,0:T(8,128)(2,1)} async-done(((bf16[128,1024]{1,0:T(8,128)(2,1)}), bf16[128,256]{1,0:T(8,128)(2,1)}) %reduce-scatter.5.cloned.1.call-update) | async-done | bytes 65552 | tf_op jit(solution)/shard_map/reduce_scatter | solution.py:52
  159.1 17.2 %all-reduce.1 = (f32[128]{0:T(128)S(1)}, f32[128,2]{1,0:T(8,128)S(1)}) all-reduce(f32[128]{0:T(128)S(1)} %get-tuple-element.56, f32[128,2]{1,0:T(8,128)S(1)} %reshape.133), channel_id=1, replica_groups=mesh['ctx'=8,'exp'=4] {'exp'}, use_global_device_ids=true, to_apply=%region_12.13 | all-reduce | flops 384 | bytes 3072 | tf_op jit(solution)/shard_map/psum | solution.py:129
  178.1 2.6 %collective-permute-start.3 = (bf16[256,15]{0,1:T(8,128)(2,1)S(1)}, bf16[256,15]{0,1:T(8,128)(2,1)S(1)}, u32[]{:S(2)}, u32[]{:S(2)}) collective-permute-start(bf16[256,15]{0,1:T(8,128)(2,1)S(1)} %get-tuple-element.69), channel_id=1, source_target_pairs={{4,0},{8,4},{12,8},{16,12},{20,16},{24,20},{28,24},{0,28},{5,1},{9... | collective-permute-start | bytes 23048 | tf_op jit(solution)/shard_map/ppermute | solution.py:18
  180.8 23.3 %all-reduce = (f32[256,31]{0,1:T(8,128)}, f32[256]{0:T(256)}) all-reduce(f32[256,31]{0,1:T(8,128)S(1)} %stack.127, f32[256]{0:T(256)S(1)} %get-tuple-element.55), channel_id=1, replica_groups=mesh['ctx'=8,'exp'=4] {'ctx'}, use_global_device_ids=true, to_apply=%region_44.45 | all-reduce | flops 8192 | bytes 65536 | tf_op jit(solution)/shard_map/psum | solution.py:147
  (199 shorter events, 35.3 us)
Async XLA Ops:
  7.2 81.0 %copy-start = (bf16[1,1024,1024]{2,1,0:T(8,128)(2,1)S(1)}, bf16[1,1024,1024]{2,1,0:T(8,128)(2,1)}, u32[]{:S(2)}) copy-start(bf16[1,1024,1024]{2,1,0:T(8,128)(2,1)} %param.14) | copy-start | bytes 6291460
  8.3 32.8 %collective-permute-start = (bf16[256,15]{0,1:T(8,128)(2,1)S(1)}, bf16[256,15]{0,1:T(8,128)(2,1)S(1)}, u32[]{:S(2)}, u32[]{:S(2)}) collective-permute-start(bf16[256,15]{0,1:T(8,128)(2,1)S(1)} %get-tuple-element.71), channel_id=1, source_target_pairs={{0,4},{4,8},{8,12},{12,16},{16,20},{20,24},{24,28},{28,0},{1,5},{5... | collective-permute-start | bytes 23048 | tf_op jit(solution)/shard_map/ppermute | solution.py:16
  8.8 32.4 %collective-permute-start.1 = (bf16[256,15]{0,1:T(8,128)(2,1)S(1)}, bf16[256,15]{0,1:T(8,128)(2,1)S(1)}, u32[]{:S(2)}, u32[]{:S(2)}) collective-permute-start(bf16[256,15]{0,1:T(8,128)(2,1)S(1)} %get-tuple-element.72), channel_id=1, source_target_pairs={{4,0},{8,4},{12,8},{16,12},{20,16},{24,20},{28,24},{0,28},{5,1},{9... | collective-permute-start | bytes 23048 | tf_op jit(solution)/shard_map/ppermute | solution.py:18
  36.7 35.1 %all-to-all-start.2 = ((bf16[8,32,1024]{2,1,0:T(8,128)(2,1)}), bf16[8,32,1024]{2,1,0:T(8,128)(2,1)}, u32[]{:S(2)}, u32[]{:S(2)}) async-start(bf16[8,32,1024]{2,1,0:T(8,128)(2,1)} %bitcast.149), calls=%async_computation.3 | async-start | bytes 1048576 | tf_op jit(solution)/shard_map/all_to_all | solution.py:91
  71.8 13.8 %all-to-all-start = ((bf16[8,32,1024]{2,1,0:T(8,128)(2,1)}), bf16[8,32,1024]{2,1,0:T(8,128)(2,1)S(1)}, u32[]{:S(2)}, u32[]{:S(2)}) async-start(bf16[8,32,1024]{2,1,0:T(8,128)(2,1)} %bitcast.36), calls=%async_computation | async-start | bytes 1048576 | tf_op jit(solution)/shard_map/all_to_all | solution.py:90
  92.5 13.2 %all-to-all-start.1 = ((bf16[8,32,1024]{2,1,0:T(8,128)(2,1)}), bf16[8,32,1024]{2,1,0:T(8,128)(2,1)S(1)}, u32[]{:S(2)}, u32[]{:S(2)}) async-start(bf16[8,32,1024]{2,1,0:T(8,128)(2,1)} %fusion.15), calls=%async_computation.1 | async-start | bytes 1048576 | tf_op jit(solution)/shard_map/all_to_all | solution.py:43
  105.6 16.2 %all-to-all-start.3 = ((bf16[8,32,1024]{2,1,0:T(8,128)(2,1)}), bf16[8,32,1024]{2,1,0:T(8,128)(2,1)}, u32[]{:S(2)}, u32[]{:S(2)}) async-start(bf16[8,32,1024]{2,1,0:T(8,128)(2,1)} %bitcast.48), calls=%async_computation.4 | async-start | bytes 1048576 | tf_op jit(solution)/shard_map/all_to_all | solution.py:43
  109.8 27.9 %reduce-scatter.3.cloned.1.call-start = ((), (), s32[]{:S(2)}) async-start(), calls=%async_computation.6 | async-start | bytes 327680 | tf_op jit(solution)/shard_map/reduce_scatter | solution.py:52
  119.6 38.6 %reduce-scatter.5.cloned.1.call-start = ((), (), s32[]{:S(2)}) async-start(), calls=%async_computation.7 | async-start | bytes 327680 | tf_op jit(solution)/shard_map/reduce_scatter | solution.py:52
  133.2 43.1 %copy-start.65 = (f32[128]{0:T(128)S(1)}, f32[128]{0:T(128)}, u32[]{:S(2)}) copy-start(f32[128]{0:T(128)} %copy-done.64) | copy-start | bytes 1540
  176.4 29.1 %copy-start.19 = (f32[256,1]{0,1:T(1,128)S(1)}, f32[256,1]{0,1:T(1,128)}, u32[]{:S(2)}) copy-start(f32[256,1]{0,1:T(1,128)} %copy-done.18) | copy-start | bytes 3076
  176.4 29.1 %copy-start.21 = (f32[256,1]{0,1:T(1,128)S(1)}, f32[256,1]{0,1:T(1,128)}, u32[]{:S(2)}) copy-start(f32[256,1]{0,1:T(1,128)} %copy-done.20) | copy-start | bytes 3076
  176.4 29.1 %copy-start.23 = (f32[256,1]{0,1:T(1,128)S(1)}, f32[256,1]{0,1:T(1,128)}, u32[]{:S(2)}) copy-start(f32[256,1]{0,1:T(1,128)} %copy-done.22) | copy-start | bytes 3076
  176.4 29.1 %copy-start.25 = (f32[256,1]{0,1:T(1,128)S(1)}, f32[256,1]{0,1:T(1,128)}, u32[]{:S(2)}) copy-start(f32[256,1]{0,1:T(1,128)} %copy-done.24) | copy-start | bytes 3076
  176.4 29.1 %copy-start.27 = (f32[256,1]{0,1:T(1,128)S(1)}, f32[256,1]{0,1:T(1,128)}, u32[]{:S(2)}) copy-start(f32[256,1]{0,1:T(1,128)} %copy-done.26) | copy-start | bytes 3076
  176.4 29.1 %copy-start.29 = (f32[256,1]{0,1:T(1,128)S(1)}, f32[256,1]{0,1:T(1,128)}, u32[]{:S(2)}) copy-start(f32[256,1]{0,1:T(1,128)} %copy-done.28) | copy-start | bytes 3076
  176.4 29.1 %copy-start.31 = (f32[256,1]{0,1:T(1,128)S(1)}, f32[256,1]{0,1:T(1,128)}, u32[]{:S(2)}) copy-start(f32[256,1]{0,1:T(1,128)} %copy-done.30) | copy-start | bytes 3076
  176.4 29.1 %copy-start.33 = (f32[256,1]{0,1:T(1,128)S(1)}, f32[256,1]{0,1:T(1,128)}, u32[]{:S(2)}) copy-start(f32[256,1]{0,1:T(1,128)} %copy-done.32) | copy-start | bytes 3076
  176.4 29.1 %copy-start.35 = (f32[256,1]{0,1:T(1,128)S(1)}, f32[256,1]{0,1:T(1,128)}, u32[]{:S(2)}) copy-start(f32[256,1]{0,1:T(1,128)} %copy-done.34) | copy-start | bytes 3076
  176.5 29.1 %copy-start.37 = (f32[256,1]{0,1:T(1,128)S(1)}, f32[256,1]{0,1:T(1,128)}, u32[]{:S(2)}) copy-start(f32[256,1]{0,1:T(1,128)} %copy-done.36) | copy-start | bytes 3076
  176.5 29.1 %copy-start.39 = (f32[256,1]{0,1:T(1,128)S(1)}, f32[256,1]{0,1:T(1,128)}, u32[]{:S(2)}) copy-start(f32[256,1]{0,1:T(1,128)} %copy-done.38) | copy-start | bytes 3076
  176.5 29.1 %copy-start.41 = (f32[256,1]{0,1:T(1,128)S(1)}, f32[256,1]{0,1:T(1,128)}, u32[]{:S(2)}) copy-start(f32[256,1]{0,1:T(1,128)} %copy-done.40) | copy-start | bytes 3076
  178.0 27.5 %collective-permute-start.2 = (bf16[256,15]{0,1:T(8,128)(2,1)S(1)}, bf16[256,15]{0,1:T(8,128)(2,1)S(1)}, u32[]{:S(2)}, u32[]{:S(2)}) collective-permute-start(bf16[256,15]{0,1:T(8,128)(2,1)S(1)} %get-tuple-element.68), channel_id=1, source_target_pairs={{0,4},{4,8},{8,12},{12,16},{16,20},{20,24},{24,28},{28,0},{1,5},{5... | collective-permute-start | bytes 23048 | tf_op jit(solution)/shard_map/ppermute | solution.py:16
  178.1 27.4 %collective-permute-start.3 = (bf16[256,15]{0,1:T(8,128)(2,1)S(1)}, bf16[256,15]{0,1:T(8,128)(2,1)S(1)}, u32[]{:S(2)}, u32[]{:S(2)}) collective-permute-start(bf16[256,15]{0,1:T(8,128)(2,1)S(1)} %get-tuple-element.69), channel_id=1, source_target_pairs={{4,0},{8,4},{12,8},{16,12},{20,16},{24,20},{28,24},{0,28},{5,1},{9... | collective-permute-start | bytes 23048 | tf_op jit(solution)/shard_map/ppermute | solution.py:18
  (52 other events, 427.1 us)
Sparse Core Ops, SparseCore 0:
  119.7 18.0 reduce-scatter.2
  140.1 17.9 reduce-scatter.4
where the time goes:
time: 215 us; the launch traced here: 214 us
  blocking collectives  81.2 us (38%)
  waiting for transfers between devices  32.6 us (15%)
  local copies, waits for them, and re-layouts  24.1 us (11%)
  starting transfers between devices  22.3 us (10%)
  matrix products  20.8 us (10%)
  other arithmetic  17.6 us (8%)
  between operations  15.1 us (7%)
    psum x1, blocking collectives, local(): grad_taps, grad_gain = lax.psum((tap_local, gain_local), 'ctx')  23.3 us
    reduce_scatter x2, waiting for transfers between devices, bring_back(): lax.psum_scatter(term.astype(jnp.bfloat16), 'exp', scatter_dimension=1, t...  21.3 us
    psum x1, blocking collectives, local(): lax.psum(jnp.sum(d_normed * gain_f[:, None] * mixed_f, axis=0), 'exp')  17.2 us
    all_gather x1, blocking collectives, local(): lax.all_gather(grad_out, 'exp', axis=0, tiled=True)  15 us
    all_gather x1, blocking collectives, local(): lax.all_gather(normed_part, 'exp', axis=0, tiled=True)  13.8 us
    psum x1, blocking collectives, local(): squares = lax.psum(jnp.sum(mixed_f * mixed_f, axis=0), 'exp')  11.9 us
    all_to_all x2, starting transfers between devices, bring_back(): lax.all_to_all(values.reshape(experts, capacity, width).astype(jnp.bfloat...  7.65 us
    gather x3, local copies, waits for them, and re-layouts, bring_back(): picked = back.reshape(experts * capacity, width)[dest]  7 us
  transfers between devices with their start and end apart: 10, of which 4 were waited for; matrix products, arithmetic and copies ran while one was open for 23% of the time, Pallas kernels for 0%

commit v1 on v0

--- a/solution.py
+++ b/solution.py
@@ -126,7 +126,9 @@
     d_share, unused_dots = bring_back(d_rows, dest, jnp.ones_like(gates), experts, capacity, None)
     d_normed = d_share.T
     gain_local = jnp.sum(d_normed * mixed_f * scale[None, :], axis=1)
-    norm_terms = lax.psum(jnp.sum(d_normed * gain_f[:, None] * mixed_f, axis=0), "exp")
+    norm_terms = jnp.sum(
+        lax.all_gather(jnp.sum(d_normed * gain_f[:, None] * mixed_f, axis=0), "exp"), axis=0
+    )
     cot_own = grad_out.astype(jnp.float32)
     d_mixed = (
         cot_own

time: 215 us -> 205 us (0.953)
  waiting for transfers between devices: 32.6 us -> 15.6 us
  blocking collectives: 81.2 us -> 88.7 us
    reduce_scatter x2, waiting for transfers between devices: 21.3 us -> 4.33 us  [bring_back(): lax.psum_scatter(term.astype(jnp.bfloat16), 'exp', scatter_dimension=1, t...]
    all_gather x0 -> x1, blocking collectives: none -> 7.91 us  [local(): lax.all_gather(jnp.sum(d_normed * gain_f[:, None] * mixed_f, axis=0), 'exp')]
  transfers between devices with their start and end apart: 10 -> 10, of which waited for: 4 -> 3; matrix products, arithmetic and copies ran while one was open for 23% -> 25% of each run, Pallas kernels for 0% -> 0%
where the time goes in v1:
time: 205 us; the launch traced here: 204 us
  blocking collectives  88.7 us (43%)
  local copies, waits for them, and re-layouts  24.1 us (12%)
  starting transfers between devices  22.3 us (11%)
  matrix products  20.8 us (10%)
  other arithmetic  17.6 us (9%)
  waiting for transfers between devices  15.6 us (8%)
  between operations  15.1 us (7%)
    psum x1, blocking collectives, local(): grad_taps, grad_gain = lax.psum((tap_local, gain_local), 'ctx')  23.4 us
    psum x1, blocking collectives, local(): grad_gates = lax.psum(gate_dots, 'exp').reshape(tokens, 2)  16.6 us
    all_gather x1, blocking collectives, local(): lax.all_gather(grad_out, 'exp', axis=0, tiled=True)  15 us
    all_gather x1, blocking collectives, local(): lax.all_gather(normed_part, 'exp', axis=0, tiled=True)  13.8 us
    psum x1, blocking collectives, local(): squares = lax.psum(jnp.sum(mixed_f * mixed_f, axis=0), 'exp')  11.9 us
    all_gather x1, blocking collectives, local(): lax.all_gather(jnp.sum(d_normed * gain_f[:, None] * mixed_f, axis=0), 'exp')  7.91 us
    all_to_all x2, starting transfers between devices, bring_back(): lax.all_to_all(values.reshape(experts, capacity, width).astype(jnp.bfloat...  7.65 us
    gather x3, local copies, waits for them, and re-layouts, bring_back(): picked = back.reshape(experts * capacity, width)[dest]  7 us
  transfers between devices with their start and end apart: 10, of which 3 were waited for; matrix products, arithmetic and copies ran while one was open for 25% of the time, Pallas kernels for 0%

profile of v1, /device:TPU:0, one launch (start us, length us, event | category | flops | bytes accessed | tf_op | source)
XLA Modules:
  0.0 204.2 jit_solution(6581926046643008269)
XLA Ops:
  8.8 2.9 %collective-permute-start.1 = (bf16[256,15]{0,1:T(8,128)(2,1)S(1)}, bf16[256,15]{0,1:T(8,128)(2,1)S(1)}, u32[]{:S(2)}, u32[]{:S(2)}) collective-permute-start(bf16[256,15]{0,1:T(8,128)(2,1)S(1)} %get-tuple-element.70), channel_id=1, source_target_pairs={{4,0},{8,4},{12,8},{16,12},{20,16},{24,20},{28,24},{0,28},{5,1},{9... | collective-permute-start | bytes 23048 | tf_op jit(solution)/shard_map/ppermute | solution.py:18
  15.5 15.0 %all_gather.13 = bf16[1024,128]{1,0:T(8,128)(2,1)S(1)} all-gather(bf16[256,128]{1,0:T(8,128)(2,1)} %param.17), channel_id=1, replica_groups=mesh['ctx'=8,'exp'=4] {'exp'}, dimensions={0}, use_global_device_ids=true | all-gather | bytes 327680 | tf_op jit(solution)/shard_map/all_gather | solution.py:79
  34.2 2.5 %scatter_custom_fusion.1 = bf16[256,1024]{1,0:T(8,128)(2,1)} fusion(s32[256]{0:T(256)S(1)} %bitcast.246, f32[256,1024]{1,0:T(8,128)S(1)} %convert_element_type.108, f32[256]{0:T(256)S(1)} %mul.828, bf16[]{:T(256)} %constant.8.clone.1), kind=kCustom, calls=%fused_computation.29 | custom fusion | flops 524288 | bytes 1573890 | tf_op jit(solution)/shard_map/scatter | solution.py:88
  36.7 4.1 %all-to-all-start.2 = ((bf16[8,32,1024]{2,1,0:T(8,128)(2,1)}), bf16[8,32,1024]{2,1,0:T(8,128)(2,1)}, u32[]{:S(2)}, u32[]{:S(2)}) async-start(bf16[8,32,1024]{2,1,0:T(8,128)(2,1)} %bitcast.150), calls=%async_computation.3 | async-start | bytes 1048576 | tf_op jit(solution)/shard_map/all_to_all | solution.py:91
  42.4 11.9 %psum.28 = f32[128]{0:T(128)S(1)} all-reduce(f32[128]{0:T(128)} %get-tuple-element.60), channel_id=1, replica_groups=mesh['ctx'=8,'exp'=4] {'exp'}, use_global_device_ids=true, to_apply=%region_4.5 | all-reduce | flops 128 | bytes 1024 | tf_op jit(solution)/shard_map/psum | solution.py:74
  54.9 13.8 %all_gather.12 = bf16[1024,128]{0,1:T(8,128)(2,1)S(1)} all-gather(bf16[256,128]{0,1:T(8,128)(2,1)S(1)} %fusion.27), channel_id=1, replica_groups=mesh['ctx'=8,'exp'=4] {'exp'}, dimensions={0}, use_global_device_ids=true | all-gather | bytes 327680 | tf_op jit(solution)/shard_map/all_gather | solution.py:78
  69.2 2.6 %scatter_custom_fusion = bf16[256,1024]{1,0:T(8,128)(2,1)} fusion(s32[256]{0:T(256)} %bitcast.247, bf16[256,1024]{1,0:T(8,128)(2,1)S(1)} %reshape.158, bf16[]{:T(256)} %constant.8.clone.1), kind=kCustom, calls=%fused_computation.41 | custom fusion | bytes 524800 | tf_op jit(solution)/shard_map/scatter | solution.py:87
  71.8 4.1 %all-to-all-start = ((bf16[8,32,1024]{2,1,0:T(8,128)(2,1)}), bf16[8,32,1024]{2,1,0:T(8,128)(2,1)S(1)}, u32[]{:S(2)}, u32[]{:S(2)}) async-start(bf16[8,32,1024]{2,1,0:T(8,128)(2,1)} %bitcast.36), calls=%async_computation | async-start | bytes 1048576 | tf_op jit(solution)/shard_map/all_to_all | solution.py:90
  76.5 3.5 %fusion.2 = f32[256,1024]{1,0:T(8,128)} fusion(bf16[256,1024]{1,0:T(8,128)(2,1)} %bitcast.47, bf16[1,1024,1024]{2,1,0:T(8,128)(2,1)} %param.16), kind=kOutput, calls=%fused_computation.6 | convolution fusion | flops 536870912 | bytes 3670016 | tf_op jit(solution)/shard_map/dot_general | solution.py:108
  80.0 5.6 %all-to-all-done = bf16[8,32,1024]{2,1,0:T(8,128)(2,1)S(1)} async-done(((bf16[8,32,1024]{2,1,0:T(8,128)(2,1)}), bf16[8,32,1024]{2,1,0:T(8,128)(2,1)S(1)}, u32[]{:S(2)}, u32[]{:S(2)}) %all-to-all-start) | async-done | bytes 524320 | tf_op jit(solution)/shard_map/all_to_all | solution.py:90
  85.6 2.5 %fusion.6 = f32[256,1024]{1,0:T(8,128)S(1)} fusion(bf16[256,1024]{1,0:T(8,128)(2,1)S(1)} %bitcast.146, bf16[1,1024,1024]{2,1,0:T(8,128)(2,1)} %param.15), kind=kOutput, calls=%fused_computation.10 | convolution fusion | flops 536870912 | bytes 3670016 | tf_op jit(solution)/shard_map/dot_general | solution.py:99
  92.5 3.5 %all-to-all-start.1 = ((bf16[8,32,1024]{2,1,0:T(8,128)(2,1)}), bf16[8,32,1024]{2,1,0:T(8,128)(2,1)S(1)}, u32[]{:S(2)}, u32[]{:S(2)}) async-start(bf16[8,32,1024]{2,1,0:T(8,128)(2,1)} %fusion.15), calls=%async_computation.1 | async-start | bytes 1048576 | tf_op jit(solution)/shard_map/all_to_all | solution.py:43
  100.0 5.7 %all-to-all-done.1 = bf16[8,32,1024]{2,1,0:T(8,128)(2,1)S(1)} async-done(((bf16[8,32,1024]{2,1,0:T(8,128)(2,1)}), bf16[8,32,1024]{2,1,0:T(8,128)(2,1)S(1)}, u32[]{:S(2)}, u32[]{:S(2)}) %all-to-all-start.1) | async-done | bytes 524320 | tf_op jit(solution)/shard_map/all_to_all | solution.py:43
  105.6 4.2 %all-to-all-start.3 = ((bf16[8,32,1024]{2,1,0:T(8,128)(2,1)}), bf16[8,32,1024]{2,1,0:T(8,128)(2,1)}, u32[]{:S(2)}, u32[]{:S(2)}) async-start(bf16[8,32,1024]{2,1,0:T(8,128)(2,1)} %bitcast.48), calls=%async_computation.4 | async-start | bytes 1048576 | tf_op jit(solution)/shard_map/all_to_all | solution.py:43
  113.3 2.9 %gather.9 = f32[128,2,1024]{2,1,0:T(2,128)} reshape(f32[256,1024]{1,0:T(8,128)} %gather_fusion) | data formatting | bytes 2097152 | tf_op jit(solution)/shard_map/gather | solution.py:50
  116.2 3.3 %multiply_reduce_fusion.1 = bf16[128,1024]{1,0:T(8,128)(2,1)} fusion(f32[128,2,1024]{2,1,0:T(2,128)} %gather.9, f32[128,2]{1,0:T(8,128)S(1)} %copy.35), kind=kLoop, calls=%fused_computation.26 | loop fusion | flops 393216 | bytes 1311744 | tf_op jit(solution)/shard_map/reduce_sum | solution.py:51
  125.0 2.9 %reshape.132 = f32[128,2,1024]{2,1,0:T(2,128)} reshape(f32[256,1024]{1,0:T(8,128)} %gather_fusion.1) | data formatting | bytes 2097152 | tf_op jit(solution)/shard_map/reshape | solution.py:51
  127.9 3.2 %reduce_sum.357 = bf16[128,1024]{1,0:T(8,128)(2,1)} reduce(f32[128,2,1024]{2,1,0:T(2,128)} %reshape.132, f32[]{:T(128)} %constant.7.clone.1), dimensions={1}, to_apply=%region_9.10 | reduce | flops 131072 | bytes 1310724 | tf_op jit(solution)/shard_map/reduce_sum | solution.py:51
  133.2 3.3 %convert_bitcast_fusion = bf16[1,1024,1024]{2,1,0:T(8,128)(2,1)} fusion(bf16[256,1024]{1,0:T(8,128)(2,1)S(1)} %copy-done.15, bf16[256,1024]{1,0:T(8,128)(2,1)} %bitcast.47), kind=kOutput, calls=%fused_computation.16 | convolution fusion | flops 537919488 | bytes 3145728 | tf_op jit(solution)/shard_map/dot_general | solution.py:111
  136.8 16.6 %psum.31 = f32[128,2]{1,0:T(8,128)S(1)} all-reduce(f32[128,2]{1,0:T(8,128)S(1)} %reshape.133), channel_id=1, replica_groups=mesh['ctx'=8,'exp'=4] {'exp'}, use_global_device_ids=true, to_apply=%region_48.49 | all-reduce | flops 256 | bytes 2048 | tf_op jit(solution)/shard_map/psum | solution.py:105
  154.1 4.3 %reduce-scatter.5.cloned.1.call-done = bf16[128,256]{1,0:T(8,128)(2,1)} async-done(((bf16[128,1024]{1,0:T(8,128)(2,1)}), bf16[128,256]{1,0:T(8,128)(2,1)}) %reduce-scatter.5.cloned.1.call-update) | async-done | bytes 65552 | tf_op jit(solution)/shard_map/reduce_scatter | solution.py:52
  159.4 7.9 %all-gather.1 = f32[4,1,128]{2,1,0:T(1,128)S(1)} all-gather(f32[1,1,128]{2,1,0:T(1,128)S(1)} %bitcast.250), channel_id=2, replica_groups=mesh['ctx'=8,'exp'=4] {'exp'}, dimensions={0}, use_global_device_ids=true | all-gather | bytes 2560 | tf_op jit(solution)/shard_map/all_gather | solution.py:130
  169.1 2.6 %collective-permute-start.3 = (bf16[256,15]{0,1:T(8,128)(2,1)S(1)}, bf16[256,15]{0,1:T(8,128)(2,1)S(1)}, u32[]{:S(2)}, u32[]{:S(2)}) collective-permute-start(bf16[256,15]{0,1:T(8,128)(2,1)S(1)} %get-tuple-element.67), channel_id=1, source_target_pairs={{4,0},{8,4},{12,8},{16,12},{20,16},{24,20},{28,24},{0,28},{5,1},{9... | collective-permute-start | bytes 23048 | tf_op jit(solution)/shard_map/ppermute | solution.py:18
  171.8 23.4 %all-reduce = (f32[256,31]{0,1:T(8,128)}, f32[256]{0:T(256)}) all-reduce(f32[256,31]{0,1:T(8,128)S(1)} %stack.127, f32[256]{0:T(256)S(1)} %get-tuple-element.55), channel_id=1, replica_groups=mesh['ctx'=8,'exp'=4] {'ctx'}, use_global_device_ids=true, to_apply=%region_44.45 | all-reduce | flops 8192 | bytes 65536 | tf_op jit(solution)/shard_map/psum | solution.py:149
  (201 shorter events, 36.7 us)
Async XLA Ops:
  7.2 81.0 %copy-start = (bf16[1,1024,1024]{2,1,0:T(8,128)(2,1)S(1)}, bf16[1,1024,1024]{2,1,0:T(8,128)(2,1)}, u32[]{:S(2)}) copy-start(bf16[1,1024,1024]{2,1,0:T(8,128)(2,1)} %param.14) | copy-start | bytes 6291460
  8.3 32.8 %collective-permute-start = (bf16[256,15]{0,1:T(8,128)(2,1)S(1)}, bf16[256,15]{0,1:T(8,128)(2,1)S(1)}, u32[]{:S(2)}, u32[]{:S(2)}) collective-permute-start(bf16[256,15]{0,1:T(8,128)(2,1)S(1)} %get-tuple-element.69), channel_id=1, source_target_pairs={{0,4},{4,8},{8,12},{12,16},{16,20},{20,24},{24,28},{28,0},{1,5},{5... | collective-permute-start | bytes 23048 | tf_op jit(solution)/shard_map/ppermute | solution.py:16
  8.8 32.4 %collective-permute-start.1 = (bf16[256,15]{0,1:T(8,128)(2,1)S(1)}, bf16[256,15]{0,1:T(8,128)(2,1)S(1)}, u32[]{:S(2)}, u32[]{:S(2)}) collective-permute-start(bf16[256,15]{0,1:T(8,128)(2,1)S(1)} %get-tuple-element.70), channel_id=1, source_target_pairs={{4,0},{8,4},{12,8},{16,12},{20,16},{24,20},{28,24},{0,28},{5,1},{9... | collective-permute-start | bytes 23048 | tf_op jit(solution)/shard_map/ppermute | solution.py:18
  36.7 35.1 %all-to-all-start.2 = ((bf16[8,32,1024]{2,1,0:T(8,128)(2,1)}), bf16[8,32,1024]{2,1,0:T(8,128)(2,1)}, u32[]{:S(2)}, u32[]{:S(2)}) async-start(bf16[8,32,1024]{2,1,0:T(8,128)(2,1)} %bitcast.150), calls=%async_computation.3 | async-start | bytes 1048576 | tf_op jit(solution)/shard_map/all_to_all | solution.py:91
  71.8 13.8 %all-to-all-start = ((bf16[8,32,1024]{2,1,0:T(8,128)(2,1)}), bf16[8,32,1024]{2,1,0:T(8,128)(2,1)S(1)}, u32[]{:S(2)}, u32[]{:S(2)}) async-start(bf16[8,32,1024]{2,1,0:T(8,128)(2,1)} %bitcast.36), calls=%async_computation | async-start | bytes 1048576 | tf_op jit(solution)/shard_map/all_to_all | solution.py:90
  92.5 13.2 %all-to-all-start.1 = ((bf16[8,32,1024]{2,1,0:T(8,128)(2,1)}), bf16[8,32,1024]{2,1,0:T(8,128)(2,1)S(1)}, u32[]{:S(2)}, u32[]{:S(2)}) async-start(bf16[8,32,1024]{2,1,0:T(8,128)(2,1)} %fusion.15), calls=%async_computation.1 | async-start | bytes 1048576 | tf_op jit(solution)/shard_map/all_to_all | solution.py:43
  105.6 16.2 %all-to-all-start.3 = ((bf16[8,32,1024]{2,1,0:T(8,128)(2,1)}), bf16[8,32,1024]{2,1,0:T(8,128)(2,1)}, u32[]{:S(2)}, u32[]{:S(2)}) async-start(bf16[8,32,1024]{2,1,0:T(8,128)(2,1)} %bitcast.48), calls=%async_computation.4 | async-start | bytes 1048576 | tf_op jit(solution)/shard_map/all_to_all | solution.py:43
  109.8 44.3 %reduce-scatter.3.cloned.1.call-start = ((), (), s32[]{:S(2)}) async-start(), calls=%async_computation.6 | async-start | bytes 327680 | tf_op jit(solution)/shard_map/reduce_scatter | solution.py:52
  119.6 38.8 %reduce-scatter.5.cloned.1.call-start = ((), (), s32[]{:S(2)}) async-start(), calls=%async_computation.7 | async-start | bytes 327680 | tf_op jit(solution)/shard_map/reduce_scatter | solution.py:52
  136.5 30.9 %copy-start.65 = (f32[128]{0:T(128)S(1)}, f32[128]{0:T(128)}, u32[]{:S(2)}) copy-start(f32[128]{0:T(128)} %copy-done.64) | copy-start | bytes 1540
  167.4 28.7 %copy-start.19 = (f32[256,1]{0,1:T(1,128)S(1)}, f32[256,1]{0,1:T(1,128)}, u32[]{:S(2)}) copy-start(f32[256,1]{0,1:T(1,128)} %copy-done.18) | copy-start | bytes 3076
  167.4 28.7 %copy-start.21 = (f32[256,1]{0,1:T(1,128)S(1)}, f32[256,1]{0,1:T(1,128)}, u32[]{:S(2)}) copy-start(f32[256,1]{0,1:T(1,128)} %copy-done.20) | copy-start | bytes 3076
  167.4 28.7 %copy-start.23 = (f32[256,1]{0,1:T(1,128)S(1)}, f32[256,1]{0,1:T(1,128)}, u32[]{:S(2)}) copy-start(f32[256,1]{0,1:T(1,128)} %copy-done.22) | copy-start | bytes 3076
  167.4 28.7 %copy-start.25 = (f32[256,1]{0,1:T(1,128)S(1)}, f32[256,1]{0,1:T(1,128)}, u32[]{:S(2)}) copy-start(f32[256,1]{0,1:T(1,128)} %copy-done.24) | copy-start | bytes 3076
  167.4 28.7 %copy-start.27 = (f32[256,1]{0,1:T(1,128)S(1)}, f32[256,1]{0,1:T(1,128)}, u32[]{:S(2)}) copy-start(f32[256,1]{0,1:T(1,128)} %copy-done.26) | copy-start | bytes 3076
  167.4 28.7 %copy-start.29 = (f32[256,1]{0,1:T(1,128)S(1)}, f32[256,1]{0,1:T(1,128)}, u32[]{:S(2)}) copy-start(f32[256,1]{0,1:T(1,128)} %copy-done.28) | copy-start | bytes 3076
  167.4 28.7 %copy-start.31 = (f32[256,1]{0,1:T(1,128)S(1)}, f32[256,1]{0,1:T(1,128)}, u32[]{:S(2)}) copy-start(f32[256,1]{0,1:T(1,128)} %copy-done.30) | copy-start | bytes 3076
  167.4 28.7 %copy-start.33 = (f32[256,1]{0,1:T(1,128)S(1)}, f32[256,1]{0,1:T(1,128)}, u32[]{:S(2)}) copy-start(f32[256,1]{0,1:T(1,128)} %copy-done.32) | copy-start | bytes 3076
  167.4 28.7 %copy-start.35 = (f32[256,1]{0,1:T(1,128)S(1)}, f32[256,1]{0,1:T(1,128)}, u32[]{:S(2)}) copy-start(f32[256,1]{0,1:T(1,128)} %copy-done.34) | copy-start | bytes 3076
  167.4 28.7 %copy-start.37 = (f32[256,1]{0,1:T(1,128)S(1)}, f32[256,1]{0,1:T(1,128)}, u32[]{:S(2)}) copy-start(f32[256,1]{0,1:T(1,128)} %copy-done.36) | copy-start | bytes 3076
  167.5 28.7 %copy-start.39 = (f32[256,1]{0,1:T(1,128)S(1)}, f32[256,1]{0,1:T(1,128)}, u32[]{:S(2)}) copy-start(f32[256,1]{0,1:T(1,128)} %copy-done.38) | copy-start | bytes 3076
  167.5 28.7 %copy-start.41 = (f32[256,1]{0,1:T(1,128)S(1)}, f32[256,1]{0,1:T(1,128)}, u32[]{:S(2)}) copy-start(f32[256,1]{0,1:T(1,128)} %copy-done.40) | copy-start | bytes 3076
  169.0 27.0 %collective-permute-start.2 = (bf16[256,15]{0,1:T(8,128)(2,1)S(1)}, bf16[256,15]{0,1:T(8,128)(2,1)S(1)}, u32[]{:S(2)}, u32[]{:S(2)}) collective-permute-start(bf16[256,15]{0,1:T(8,128)(2,1)S(1)} %get-tuple-element.66), channel_id=1, source_target_pairs={{0,4},{4,8},{8,12},{12,16},{16,20},{20,24},{24,28},{28,0},{1,5},{5... | collective-permute-start | bytes 23048 | tf_op jit(solution)/shard_map/ppermute | solution.py:16
  169.1 26.9 %collective-permute-start.3 = (bf16[256,15]{0,1:T(8,128)(2,1)S(1)}, bf16[256,15]{0,1:T(8,128)(2,1)S(1)}, u32[]{:S(2)}, u32[]{:S(2)}) collective-permute-start(bf16[256,15]{0,1:T(8,128)(2,1)S(1)} %get-tuple-element.67), channel_id=1, source_target_pairs={{4,0},{8,4},{12,8},{16,12},{20,16},{24,20},{28,24},{0,28},{5,1},{9... | collective-permute-start | bytes 23048 | tf_op jit(solution)/shard_map/ppermute | solution.py:18
  (52 other events, 423.0 us)
Sparse Core Ops, SparseCore 0:
  119.7 18.0 reduce-scatter.2
  140.1 18.2 reduce-scatter.4
